TPU v7x, 32 devices: a whole 2x2x4 slice. The times are simulated.
32 devices in a mesh: groups: 2 (over x), tensor: 16 (over z, y, core).
Axes of the slice: x: 2, y: 2, z: 4, core: 2. Of those that a mesh axis runs over, the one named last changes fastest.
Arguments:
- residual: bfloat16 [64, 8192], P(('groups', 'tensor')), parts along dimension 0, may hold values from -6 to 6
- context: bfloat16 [64, 2048], P('groups', 'tensor'), parts along dimension 0, may hold values from -6 to 6
- w_out: bfloat16 [2048, 8192], P('tensor'), may hold values from -0.125 to 0.125
- ffn_gain: bfloat16 [8192], replicated, may hold values from 0.099609375 to 1.8984375
- w_gate: bfloat16 [8192, 3584], P(None, 'tensor'), may hold values from -0.0625 to 0.0625
- w_up: bfloat16 [8192, 3584], P(None, 'tensor'), may hold values from -0.0625 to 0.0625
- w_down: bfloat16 [3584, 8192], P('tensor'), may hold values from -0.09375 to 0.09375
Outputs:
- layer_out: bfloat16 [64, 8192], P(('groups', 'tensor')), parts along dimension 0
There are 2 independent parts, one for each index of `groups`. A program takes and returns all parts, laid end to end along the dimension named above; an argument that names none is the same for every part. Nothing has to cross between parts.
All inputs are finite; a program needn't handle non-finite values. Where the computation divides by a largest or mean magnitude, that divisor is 1e-20 or more.
Results may differ from a plain program's by a relative error of at most 0.018.
Values may be sent and summed in bfloat16 or wider, within the bound.
A program may use at most 128 MiB of HBM per device.

v0:
```python
import math

import jax
import jax.numpy as jnp
from jax import lax
from jax.sharding import PartitionSpec as P

BLOCK = 128


CLIP_LEVEL = 3.0
SCALE_EPS = 1e-06
NORM_EPS = 1e-05


def sylvester(block_order):
    hadamard = jnp.ones((1, 1), jnp.float32)
    while hadamard.shape[0] < block_order:
        upper = jnp.concatenate([hadamard, hadamard], axis=1)
        lower = jnp.concatenate([hadamard, -hadamard], axis=1)
        hadamard = jnp.concatenate([upper, lower], axis=0)
    return hadamard


def rotate(values):
    row_count = values.shape[0]
    hadamard = jnp.asarray(sylvester(BLOCK), jnp.bfloat16)
    flat = values.reshape(-1, BLOCK)
    high_part = flat.astype(jnp.bfloat16)
    low_part = (flat - high_part.astype(jnp.float32)).astype(jnp.bfloat16)
    turned = jnp.dot(high_part, hadamard, preferred_element_type=jnp.float32)
    turned = turned + jnp.dot(low_part, hadamard, preferred_element_type=jnp.float32)
    turned = turned * (1.0 / math.sqrt(BLOCK))
    return turned.reshape(row_count, -1)


def encode(values):
    row_count = values.shape[0]
    turned = rotate(values).reshape(row_count, -1, BLOCK)
    code_scales = (jnp.mean(jnp.abs(turned), axis=-1) + SCALE_EPS).astype(jnp.bfloat16)
    code_values = jnp.clip(
        turned / code_scales.astype(jnp.float32)[..., None], -CLIP_LEVEL, CLIP_LEVEL
    ).astype(jnp.bfloat16)
    return (code_values.reshape(row_count, -1), code_scales)


def dequant(code_values, code_scales):
    reshaped = code_values.astype(jnp.float32).reshape(
        code_values.shape[:-1] + (code_scales.shape[-1], BLOCK)
    )
    return reshaped * code_scales.astype(jnp.float32)[..., None]


def owner_sum(got_values, got_scales):
    summed = jnp.sum(dequant(got_values, got_scales), axis=0)
    return rotate(summed.reshape(summed.shape[0], -1))


def expand(code_values, code_scales):
    row_count = code_values.shape[0]
    hadamard = jnp.asarray(sylvester(BLOCK), jnp.bfloat16)
    mixed_rows = jnp.dot(
        code_values.reshape(-1, BLOCK), hadamard, preferred_element_type=jnp.float32
    )
    mixed_rows = mixed_rows.reshape(row_count, -1, BLOCK)
    factor = code_scales.astype(jnp.float32)[..., None] / math.sqrt(BLOCK)
    return (mixed_rows * factor).reshape(row_count, -1).astype(jnp.bfloat16)


def normalize(mid, ffn_gain):
    widened = mid.astype(jnp.float32)
    inverse = lax.rsqrt(jnp.mean(widened * widened, axis=-1, keepdims=True) + NORM_EPS)
    return widened * inverse * ffn_gain.astype(jnp.float32)


def ffn_partial(rows_in, w_gate, w_up, w_down):
    gate_part = jnp.dot(rows_in, w_gate, preferred_element_type=jnp.float32)
    up_part = jnp.dot(rows_in, w_up, preferred_element_type=jnp.float32)
    hidden = (jax.nn.silu(gate_part) * up_part).astype(jnp.bfloat16)
    return jnp.dot(hidden, w_down, preferred_element_type=jnp.float32)


def local(residual, context, w_out, ffn_gain, w_gate, w_up, w_down):
    axis_count = lax.axis_size("tensor")
    own_rows = residual.shape[0]
    model_width = residual.shape[1]
    attn_term = jnp.dot(context, w_out, preferred_element_type=jnp.float32)
    code_values, code_scales = encode(attn_term)
    got_values, got_scales = (
        lax.all_to_all(
            code_values.reshape(axis_count, own_rows, model_width),
            "tensor",
            split_axis=0,
            concat_axis=0,
            tiled=True,
        ),
        lax.all_to_all(
            code_scales.reshape(axis_count, own_rows, -1),
            "tensor",
            split_axis=0,
            concat_axis=0,
            tiled=True,
        ),
    )
    attn_back = owner_sum(got_values, got_scales)
    mid = (residual.astype(jnp.float32) + attn_back).astype(jnp.bfloat16)
    norm_values, norm_scales = encode(normalize(mid, ffn_gain))
    all_values, all_scales = (
        lax.all_gather(norm_values, "tensor", axis=0, tiled=True),
        lax.all_gather(norm_scales, "tensor", axis=0, tiled=True),
    )
    ffn_in = expand(all_values, all_scales)
    ffn_term = ffn_partial(ffn_in, w_gate, w_up, w_down)
    term_values, term_scales = encode(ffn_term)
    back_values, back_scales = (
        lax.all_to_all(
            term_values.reshape(axis_count, own_rows, model_width),
            "tensor",
            split_axis=0,
            concat_axis=0,
            tiled=True,
        ),
        lax.all_to_all(
            term_scales.reshape(axis_count, own_rows, -1),
            "tensor",
            split_axis=0,
            concat_axis=0,
            tiled=True,
        ),
    )
    ffn_back = owner_sum(back_values, back_scales)
    return (mid.astype(jnp.float32) + ffn_back).astype(jnp.bfloat16)


def solution(mesh):
    return jax.shard_map(
        local,
        mesh=mesh,
        in_specs=(
            P(("groups", "tensor"), None),
            P("groups", "tensor"),
            P("tensor", None),
            P(),
            P(None, "tensor"),
            P(None, "tensor"),
            P("tensor", None),
        ),
        out_specs=P(("groups", "tensor"), None),
        check_vma=False,
    )
```

profile of v0, /device:TPU:0, one launch (start us, length us, event | category | flops | bytes accessed | tf_op | source)
XLA Modules:
  0.0 140.9 jit_solution(2249111931305860930)
XLA Ops:
  0.0 1.6 %copy-done = bf16[128,8192]{1,0:T(8,128)(2,1)S(1)} copy-done((bf16[128,8192]{1,0:T(8,128)(2,1)S(1)}, bf16[128,8192]{1,0:T(8,128)(2,1)}, u32[]{:S(2)}) %copy-start) | copy-done | bytes 2097176
  1.6 2.1 %fusion.42 = f32[32,8192]{1,0:T(8,128)} fusion(bf16[32,128]{1,0:T(8,128)(2,1)} %param.8, bf16[128,8192]{1,0:T(8,128)(2,1)S(1)} %copy-done), kind=kOutput, calls=%fused_computation.71 | convolution fusion | flops 67108864 | bytes 3153920 | tf_op jit(solution)/shard_map/dot_general | solution.py:87
  3.7 1.4 reshape.114
  5.4 1.4 abs_reduce_fusion.1
  7.5 7.4 %all-to-all-start.1 = ((bf16[16,2,64]{2,1,0:T(2,128)(2,1)}), bf16[16,2,64]{2,1,0:T(2,128)(2,1)S(1)}, u32[]{:S(2)}, u32[]{:S(2)}) async-start(bf16[16,2,64]{2,1,0:T(2,128)(2,1)} %convert_element_type.167), calls=%async_computation.1 | async-start | bytes 16384 | tf_op jit(solution)/shard_map/all_to_all | solution.py:97
  15.0 1.3 div.59
  16.3 2.8 %div.60 = f32[16,2,8192]{2,1,0:T(2,128)} reshape(f32[32,64,128]{2,1,0:T(8,128)} %div.59) | data formatting | bytes 2097152 | tf_op jit(solution)/shard_map/div | solution.py:42
  19.1 1.4 copy.14
  20.5 1.8 %reshape_reshape.17 = f32[16,2,8192]{2,1,0:T(2,128)S(1)} reshape(f32[2048,128]{1,0:T(8,128)} %copy.14) | data formatting | bytes 2097152 | tf_op jit(solution)/shard_map/reshape;reshape | solution.py:39
  22.3 2.7 %clamp_convert_fusion.1 = bf16[16,2,8192]{2,1,0:T(2,128)(2,1)} fusion(f32[16,2,8192]{2,1,0:T(2,128)S(1)} %reshape_reshape.17, f32[16,2,8192]{2,1,0:T(2,128)} %div.60), kind=kLoop, calls=%fused_computation.20 | loop fusion | flops 786432 | bytes 2621440 | tf_op jit(solution)/shard_map/convert_element_type | solution.py:43
  25.0 6.2 %all-to-all-start = ((bf16[16,2,8192]{2,1,0:T(2,128)(2,1)}), bf16[16,2,8192]{2,1,0:T(2,128)(2,1)}, u32[]{:S(2)}, u32[]{:S(2)}) async-start(bf16[16,2,8192]{2,1,0:T(2,128)(2,1)} %clamp_convert_fusion.1), calls=%async_computation | async-start | bytes 1048576 | tf_op jit(solution)/shard_map/all_to_all | solution.py:90
  32.6 1.8 %mul.73 = f32[16,2,8192]{2,1,0:T(2,128)S(1)} reshape(f32[16,2,64,128]{3,2,1,0:T(8,128)} %mul.72) | data formatting | bytes 2097152 | tf_op jit(solution)/shard_map/mul | solution.py:51
  34.4 11.3 %all-to-all-done = bf16[16,2,8192]{2,1,0:T(2,128)(2,1)} async-done(((bf16[16,2,8192]{2,1,0:T(2,128)(2,1)}), bf16[16,2,8192]{2,1,0:T(2,128)(2,1)}, u32[]{:S(2)}, u32[]{:S(2)}) %all-to-all-start) | async-done | bytes 524320 | tf_op jit(solution)/shard_map/all_to_all | solution.py:90
  45.8 1.6 %multiply_reduce_fusion.1 = f32[2,8192]{1,0:T(2,128)S(1)} fusion(f32[16,2,8192]{2,1,0:T(2,128)S(1)} %mul.73, bf16[16,2,8192]{2,1,0:T(2,128)(2,1)} %all-to-all-done), kind=kLoop, calls=%fused_computation.19 | loop fusion | flops 770048 | bytes 1638400 | tf_op jit(solution)/shard_map/reduce_sum | solution.py:55
  48.9 21.3 %all-gather = bf16[16,2,8192]{2,1,0:T(2,128)(2,1)S(1)} all-gather(bf16[1,2,8192]{2,1,0:T(2,128)(2,1)S(1)} %fusion.29), channel_id=1, replica_groups=mesh['groups'=2,'tensor'=16] {'tensor'}, dimensions={0}, use_global_device_ids=true | all-gather | bytes 557056 | tf_op jit(solution)/shard_map/all_gather | solution.py:109
  70.6 17.5 %all-gather.1 = bf16[16,2,64]{2,1,0:T(2,128)(2,1)S(1)} all-gather(bf16[1,2,64]{2,1,0:T(2,128)(2,1)S(1)} %reshape.123), channel_id=1, replica_groups=mesh['groups'=2,'tensor'=16] {'tensor'}, dimensions={0}, use_global_device_ids=true | all-gather | bytes 4352 | tf_op jit(solution)/shard_map/all_gather | solution.py:110
  88.5 3.3 %fusion.10 = f32[32,224]{1,0:T(8,128)S(1)} fusion(bf16[8192,224]{0,1:T(8,128)(2,1)} %param.11, bf16[4,8,64,128]{3,2,1,0:T(8,128)(2,1)S(1)} %bitcast.40), kind=kOutput, calls=%fused_computation.24 | convolution fusion | flops 117440512 | bytes 4222976 | tf_op jit(solution)/shard_map/dot_general | solution.py:77
  91.8 6.7 %fusion.7 = f32[32,8192]{1,0:T(8,128)} fusion(bf16[224,8192]{1,0:T(8,128)(2,1)} %param.13, bf16[8192,224]{0,1:T(8,128)(2,1)} %param.12, bf16[4,8,64,128]{3,2,1,0:T(8,128)(2,1)S(1)} %bitcast.41, f32[32,224]{1,0:T(8,128)S(1)} %fusion.10), kind=kOutput, calls=%fused_computation.14 | convolution fusion | flops 234924032 | bytes 8941568 | tf_op jit(solution)/shard_map/dot_general | solution.py:80
  98.5 1.4 reshape.117
  100.2 1.4 abs_reduce_fusion
  102.4 1.3 div.72
  103.7 2.8 %div.73 = f32[16,2,8192]{2,1,0:T(2,128)} reshape(f32[32,64,128]{2,1,0:T(8,128)} %div.72) | data formatting | bytes 2097152 | tf_op jit(solution)/shard_map/div | solution.py:42
  106.5 1.4 copy.17
  107.9 1.8 %reshape_reshape.20 = f32[16,2,8192]{2,1,0:T(2,128)S(1)} reshape(f32[2048,128]{1,0:T(8,128)} %copy.17) | data formatting | bytes 2097152 | tf_op jit(solution)/shard_map/reshape;reshape | solution.py:39
  109.7 3.5 %all-to-all-start.3 = ((bf16[16,2,64]{2,1,0:T(2,128)(2,1)}), bf16[16,2,64]{2,1,0:T(2,128)(2,1)S(1)}, u32[]{:S(2)}, u32[]{:S(2)}) async-start(bf16[16,2,64]{2,1,0:T(2,128)(2,1)} %convert_element_type.194), calls=%async_computation.3 | async-start | bytes 16384 | tf_op jit(solution)/shard_map/all_to_all | solution.py:123
  113.2 2.7 %clamp_convert_fusion = bf16[16,2,8192]{2,1,0:T(2,128)(2,1)} fusion(f32[16,2,8192]{2,1,0:T(2,128)S(1)} %reshape_reshape.20, f32[16,2,8192]{2,1,0:T(2,128)} %div.73), kind=kLoop, calls=%fused_computation.16 | loop fusion | flops 786432 | bytes 2621440 | tf_op jit(solution)/shard_map/convert_element_type | solution.py:43
  115.9 3.6 %all-to-all-done.3 = bf16[16,2,64]{2,1,0:T(2,128)(2,1)S(1)} async-done(((bf16[16,2,64]{2,1,0:T(2,128)(2,1)}), bf16[16,2,64]{2,1,0:T(2,128)(2,1)S(1)}, u32[]{:S(2)}, u32[]{:S(2)}) %all-to-all-start.3) | async-done | bytes 4128 | tf_op jit(solution)/shard_map/all_to_all | solution.py:123
  119.5 4.2 %all-to-all-start.2 = ((bf16[16,2,8192]{2,1,0:T(2,128)(2,1)}), bf16[16,2,8192]{2,1,0:T(2,128)(2,1)}, u32[]{:S(2)}, u32[]{:S(2)}) async-start(bf16[16,2,8192]{2,1,0:T(2,128)(2,1)} %clamp_convert_fusion), calls=%async_computation.2 | async-start | bytes 1048576 | tf_op jit(solution)/shard_map/all_to_all | solution.py:116
  123.7 1.3 mul.87
  125.0 1.8 %mul.88 = f32[16,2,8192]{2,1,0:T(2,128)S(1)} reshape(f32[16,2,64,128]{3,2,1,0:T(8,128)} %mul.87) | data formatting | bytes 2097152 | tf_op jit(solution)/shard_map/mul | solution.py:51
  126.9 11.3 %all-to-all-done.2 = bf16[16,2,8192]{2,1,0:T(2,128)(2,1)} async-done(((bf16[16,2,8192]{2,1,0:T(2,128)(2,1)}), bf16[16,2,8192]{2,1,0:T(2,128)(2,1)}, u32[]{:S(2)}, u32[]{:S(2)}) %all-to-all-start.2) | async-done | bytes 524320 | tf_op jit(solution)/shard_map/all_to_all | solution.py:116
  138.2 1.6 %multiply_reduce_fusion = f32[2,8192]{1,0:T(2,128)S(1)} fusion(f32[16,2,8192]{2,1,0:T(2,128)S(1)} %mul.88, bf16[16,2,8192]{2,1,0:T(2,128)(2,1)} %all-to-all-done.2), kind=kLoop, calls=%fused_computation.15 | loop fusion | flops 770048 | bytes 1638400 | tf_op jit(solution)/shard_map/reduce_sum | solution.py:55
  (48 shorter events, 6.8 us)
Async XLA Ops:
  0.0 1.6 %copy-start = (bf16[128,8192]{1,0:T(8,128)(2,1)S(1)}, bf16[128,8192]{1,0:T(8,128)(2,1)}, u32[]{:S(2)}) copy-start(bf16[128,8192]{1,0:T(8,128)(2,1)} %param.9) | copy-start | bytes 6291460
  0.0 5.1 %copy-start.3 = (bf16[128,128]{1,0:T(8,128)(2,1)S(1)}, bf16[128,128]{1,0:T(8,128)(2,1)}, u32[]{:S(2)}) copy-start(bf16[128,128]{1,0:T(8,128)(2,1)} %constant.11.clone.1) | copy-start | bytes 98308
  6.8 12.3 %copy-start.1 = (f32[2048,128]{0,1:T(8,128)S(1)}, f32[2048,128]{0,1:T(8,128)}, u32[]{:S(2)}) copy-start(f32[2048,128]{0,1:T(8,128)} %get-tuple-element.10) | copy-start | bytes 3145732
  7.5 17.5 %all-to-all-start.1 = ((bf16[16,2,64]{2,1,0:T(2,128)(2,1)}), bf16[16,2,64]{2,1,0:T(2,128)(2,1)S(1)}, u32[]{:S(2)}, u32[]{:S(2)}) async-start(bf16[16,2,64]{2,1,0:T(2,128)(2,1)} %convert_element_type.167), calls=%async_computation.1 | async-start | bytes 16384 | tf_op jit(solution)/shard_map/all_to_all | solution.py:97
  19.1 12.1 %copy-start.6 = (bf16[8192]{0:T(1024)(128)(2,1)S(1)}, bf16[8192]{0:T(1024)(128)(2,1)}, u32[]{:S(2)}) copy-start(bf16[8192]{0:T(1024)(128)(2,1)} %param.10) | copy-start | bytes 49156
  25.0 22.8 %copy-start.5 = (bf16[2,8192]{1,0:T(2,128)(2,1)S(1)}, bf16[2,8192]{1,0:T(2,128)(2,1)}, u32[]{:S(2)}) copy-start(bf16[2,8192]{1,0:T(2,128)(2,1)} %param.7) | copy-start | bytes 98308
  25.0 20.7 %all-to-all-start = ((bf16[16,2,8192]{2,1,0:T(2,128)(2,1)}), bf16[16,2,8192]{2,1,0:T(2,128)(2,1)}, u32[]{:S(2)}, u32[]{:S(2)}) async-start(bf16[16,2,8192]{2,1,0:T(2,128)(2,1)} %clamp_convert_fusion.1), calls=%async_computation | async-start | bytes 1048576 | tf_op jit(solution)/shard_map/all_to_all | solution.py:90
  32.6 55.6 %copy-start.4 = (bf16[128,128,1]{1,0,2:T(8,128)(2,1)S(1)}, bf16[128,128,1]{1,0,2:T(8,128)(2,1)}, u32[]{:S(2)}) copy-start(bf16[128,128,1]{1,0,2:T(8,128)(2,1)} %constant.31) | copy-start | bytes 98308
  101.6 4.9 %copy-start.2 = (f32[2048,128]{0,1:T(8,128)S(1)}, f32[2048,128]{0,1:T(8,128)}, u32[]{:S(2)}) copy-start(f32[2048,128]{0,1:T(8,128)} %get-tuple-element.14) | copy-start | bytes 3145732
  109.7 9.8 %all-to-all-start.3 = ((bf16[16,2,64]{2,1,0:T(2,128)(2,1)}), bf16[16,2,64]{2,1,0:T(2,128)(2,1)S(1)}, u32[]{:S(2)}, u32[]{:S(2)}) async-start(bf16[16,2,64]{2,1,0:T(2,128)(2,1)} %convert_element_type.194), calls=%async_computation.3 | async-start | bytes 16384 | tf_op jit(solution)/shard_map/all_to_all | solution.py:123
  119.5 18.7 %all-to-all-start.2 = ((bf16[16,2,8192]{2,1,0:T(2,128)(2,1)}), bf16[16,2,8192]{2,1,0:T(2,128)(2,1)}, u32[]{:S(2)}, u32[]{:S(2)}) async-start(bf16[16,2,8192]{2,1,0:T(2,128)(2,1)} %clamp_convert_fusion), calls=%async_computation.2 | async-start | bytes 1048576 | tf_op jit(solution)/shard_map/all_to_all | solution.py:116
where the time goes:
time: 142 us; the launch traced here: 141 us
  blocking collectives  38.8 us (27%)
  local copies, waits for them, and re-layouts  27.7 us (20%)
  waiting for transfers between devices  26.2 us (18%)
  starting transfers between devices  21.3 us (15%)
  matrix products  16.8 us (12%)
  other arithmetic  9.8 us (7%)
    all_gather x1, blocking collectives, local(): lax.all_gather(norm_values, 'tensor', axis=0, tiled=True)  21.3 us
    all_gather x1, blocking collectives, local(): lax.all_gather(norm_scales, 'tensor', axis=0, tiled=True)  17.5 us
    all_to_all x1, waiting for transfers between devices, local(): lax.all_to_all(code_values.reshape(axis_count, own_rows, model_width), 't...  11.3 us
    all_to_all x1, waiting for transfers between devices, local(): lax.all_to_all(term_values.reshape(axis_count, own_rows, model_width), 't...  11.3 us
    div x4, local copies, waits for them, and re-layouts, encode(): turned / code_scales.astype(jnp.float32)[..., None]  8.27 us
    all_to_all x1, starting transfers between devices, local(): lax.all_to_all(code_scales.reshape(axis_count, own_rows, -1), 'tensor', s...  7.39 us
    dot_general x1, matrix products, ffn_partial(): return jnp.dot(hidden, w_down, preferred_element_type=jnp.float32)  6.72 us
    mul x4, local copies, waits for them, and re-layouts, dequant(): return reshaped * code_scales.astype(jnp.float32)[..., None]  6.27 us
  transfers between devices with their start and end apart: 4, of which 3 were waited for; matrix products, arithmetic and copies ran while one was open for 14% of the time, Pallas kernels for 0%

commit v1 on v0

v1 whole, which is shorter than its diff:
```python
import functools
import math

import jax
import jax.numpy as jnp
from jax import lax
from jax.experimental import pallas as pl
from jax.experimental.pallas import tpu as pltpu
from jax.sharding import PartitionSpec as P

BLOCK = 128
CLIP_LEVEL = 3.0
SCALE_EPS = 1e-06
NORM_EPS = 1e-05
CHUNKS = 4
PARTS = 2
MESH = pl.DeviceIdType.MESH
F32 = jnp.float32
BF16 = jnp.bfloat16
ROOT = 1.0 / math.sqrt(BLOCK)


def kernel(
    n, own, rows, blocks,
    res_ref, ctx_ref, wo_hbm, gain_ref, wg_hbm, wu_hbm, wd_hbm,
    out_ref,
    wo, wg, wu, wd, turn, s1, r1, s2, r2, s3, r3, resid, mid_ref, gath, lhs,
    wsem, s1s, s1r, s2s, s2r, s3s, s3r, gzs, gzr, gys, gyr, gcs, gcr,
):
    nh, nq = n // 2, n // 4
    bpc = blocks // CHUNKS
    cw = bpc * BLOCK
    per = own * bpc
    me = lax.axis_index("tensor")
    c = lax.rem(me, 2)
    y = lax.rem(me // 2, 2)
    q = me // 4
    core_dev = me + 1 - 2 * c
    y_dev = me + 2 - 4 * y

    def z_dev(k):
        return lax.rem(q + k, nq) * 4 + y * 2 + c

    def z_src(k):
        return lax.rem(q + nq - k, nq)

    wcopies = []
    for k in range(CHUNKS):
        cols = pl.ds(k * cw, cw)
        wcopies.append(pltpu.make_async_copy(wo_hbm.at[:, cols], wo.at[:, cols], wsem.at[k]))
    wcopies.append(pltpu.make_async_copy(wg_hbm, wg, wsem.at[CHUNKS]))
    wcopies.append(pltpu.make_async_copy(wu_hbm, wu, wsem.at[CHUNKS + 1]))
    wcopies.append(pltpu.make_async_copy(wd_hbm, wd, wsem.at[CHUNKS + 2]))
    for cp in wcopies:
        cp.start()

    barrier = pltpu.get_barrier_semaphore()
    for dev in [core_dev, y_dev] + [z_dev(k) for k in range(1, nq)]:
        pl.semaphore_signal(barrier, inc=1, device_id={"tensor": dev}, device_id_type=MESH)

    par = lax.broadcasted_iota(jnp.int32, (2 * BLOCK, BLOCK), 0) & lax.broadcasted_iota(
        jnp.int32, (2 * BLOCK, BLOCK), 1
    )
    par = par ^ (par >> 4)
    par = par ^ (par >> 2)
    par = par ^ (par >> 1)
    had2 = (1 - 2 * (par & 1)).astype(F32).astype(BF16)
    had = had2[:BLOCK]
    ones = jnp.ones((BLOCK, BLOCK), BF16)

    def rotate(v):
        high = v.astype(BF16)
        low = (v - high.astype(F32)).astype(BF16)
        return jnp.dot(jnp.concatenate([high, low], axis=1), had2, preferred_element_type=F32) * ROOT

    def coded(v):
        t = rotate(v)
        total = jnp.dot(jnp.abs(t).astype(BF16), ones, preferred_element_type=F32)
        scale = (total * (1.0 / BLOCK) + SCALE_EPS).astype(BF16).astype(F32)
        bound = scale * CLIP_LEVEL
        return jnp.clip(t, -bound, bound)

    sends = []

    def remote(src, dst, ssem, rsem, dev):
        cp = pltpu.make_async_remote_copy(
            src_ref=src, dst_ref=dst, send_sem=ssem, recv_sem=rsem,
            device_id={"tensor": dev}, device_id_type=MESH,
        )
        cp.start()
        sends.append(cp)
        return cp

    def term(p, k, left, w):
        x = jnp.dot(left, w[:, k * cw:(k + 1) * cw], preferred_element_type=F32)
        x = jnp.concatenate([x[:, b * BLOCK:(b + 1) * BLOCK] for b in range(bpc)], axis=0)
        v = coded(x)
        base = (k % 2) * rows * bpc
        for b in range(bpc):
            turn[pl.ds(base + b, rows, stride=bpc), :] = v[b * rows:(b + 1) * rows]
        for t in range(n):
            slot = (t % 2) * nh + (t // 2 % 2) * nq + t // 4
            s1[p, k, slot] = turn[base + t * per:base + (t + 1) * per, :].astype(BF16)

    def reduce_scatter(p, left, w, before):
        c1, c2, c3 = {}, {}, {}
        for step in range(CHUNKS + 2):
            k = step
            if k < CHUNKS:
                before(k)
                term(p, k, left, w)
                if p == 0 and k == 0:
                    pl.semaphore_wait(barrier, 1 + nq)
                c1[k] = remote(s1.at[p, k, pl.ds((1 - c) * nh, nh)], r1.at[p, k],
                               s1s.at[p, k], s1r.at[p, k], core_dev)
            k = step - 1
            if 0 <= k < CHUNKS:
                c1[k].wait_recv()
                s2[p, k] = (s1[p, k, pl.ds(c * nh, nh)].astype(F32) + r1[p, k].astype(F32)).astype(BF16)
                c2[k] = remote(s2.at[p, k, pl.ds((1 - y) * nq, nq)], r2.at[p, k],
                               s2s.at[p, k], s2r.at[p, k], y_dev)
            k = step - 2
            if 0 <= k < CHUNKS:
                c2[k].wait_recv()
                s3[p, k] = (s2[p, k, pl.ds(y * nq, nq)].astype(F32) + r2[p, k].astype(F32)).astype(BF16)
                for j in range(1, nq):
                    c3[k, j] = remote(s3.at[p, k, lax.rem(q + j, nq)], r3.at[p, k, j],
                                      s3s.at[p, k, j], s3r.at[p, k, j], z_dev(j))
        totals = []
        for k in range(CHUNKS):
            total = s3[p, k, q].astype(F32)
            for j in range(1, nq):
                c3[k, j].wait_recv()
                total = total + r3[p, k, j].astype(F32)
            totals.append(total)
        return jnp.concatenate(totals, axis=0)

    def before_out(k):
        wcopies[k].wait()

    res = res_ref[...].astype(F32)
    for b in range(blocks):
        resid[pl.ds((b // bpc) * per + b % bpc, own, stride=bpc), :] = res[:, b * BLOCK:(b + 1) * BLOCK]

    attn = reduce_scatter(0, ctx_ref[...], wo, before_out)
    mid = (resid[...] + rotate(attn)).astype(BF16).astype(F32)
    mid_ref[...] = mid
    mid4 = mid.reshape(CHUNKS, own, bpc, BLOCK)
    gain = gain_ref[...].astype(F32).reshape(CHUNKS, 1, bpc, BLOCK)
    squares = jnp.sum(jnp.sum(mid4 * mid4, axis=0), axis=(1, 2), keepdims=True)
    inverse = lax.rsqrt(squares * (1.0 / (blocks * BLOCK)) + NORM_EPS)
    normed = (mid4 * inverse[None] * gain).reshape(blocks * own, BLOCK)
    ffn_in = jnp.dot(coded(normed).astype(BF16), had, preferred_element_type=F32) * ROOT
    piece = own * blocks // PARTS
    cz, cy, cc = {}, {}, {}

    def share(a, slot, dev, ss, rs, i):
        return remote(gath.at[a, slot], gath.at[a, slot], ss.at[a, i], rs.at[a, i], dev)

    for a in range(PARTS):
        gath[a, me] = ffn_in[a * piece:(a + 1) * piece].astype(BF16)
        for k in range(1, nq):
            cz[a, k] = share(a, me, z_dev(k), gzs, gzr, k)
        cy[a, 0] = share(a, me, y_dev, gys, gyr, 0)
        cc[a, 0] = share(a, me, core_dev, gcs, gcr, 0)
    for a in range(PARTS):
        for k in range(1, nq):
            cz[a, k].wait_recv()
            slot = z_src(k) * 4 + y * 2 + c
            cy[a, k] = share(a, slot, y_dev, gys, gyr, k)
            cc[a, k] = share(a, slot, core_dev, gcs, gcr, k)
    for a in range(PARTS):
        for k in range(nq):
            cy[a, k].wait_recv()
            slot = z_src(k) * 4 + (1 - y) * 2 + c
            cc[a, nq + k] = share(a, slot, core_dev, gcs, gcr, nq + k)
    wcopies[CHUNKS].wait()
    wcopies[CHUNKS + 1].wait()
    gate = up = None
    group = CHUNKS // PARTS
    for a in range(PARTS):
        for k in range(nh):
            cc[a, k].wait_recv()
        for g in range(group):
            k = a * group + g
            base = k * rows * bpc
            for t in range(n):
                lhs[base + t * per:base + (t + 1) * per, :] = gath[a, t, g * per:(g + 1) * per, :].astype(F32)
            left = jnp.concatenate(
                [lhs[pl.ds(base + b, rows, stride=bpc), :].astype(BF16) for b in range(bpc)], axis=1
            )
            span = pl.ds(k * cw, cw)
            g_part = jnp.dot(left, wg[span, :], preferred_element_type=F32)
            u_part = jnp.dot(left, wu[span, :], preferred_element_type=F32)
            gate = g_part if gate is None else gate + g_part
            up = u_part if up is None else up + u_part
    hidden = (gate / (1.0 + jnp.exp(-gate)) * up).astype(BF16)

    def before_down(k):
        if k == 0:
            wcopies[CHUNKS + 2].wait()

    ffn = reduce_scatter(1, hidden, wd, before_down)
    resid[...] = mid_ref[...] + rotate(ffn)
    for b in range(blocks):
        row = resid[pl.ds((b // bpc) * per + b % bpc, own, stride=bpc), :]
        out_ref[:, b * BLOCK:(b + 1) * BLOCK] = row.astype(BF16)
    for cp in sends:
        cp.wait_send()


def local(residual, context, w_out, ffn_gain, w_gate, w_up, w_down):
    n = lax.axis_size("tensor")
    own, width = residual.shape
    rows = context.shape[0]
    blocks = width // BLOCK
    units = w_gate.shape[1]
    nh, nq = n // 2, n // 4
    per = own * blocks // CHUNKS
    piece = own * blocks // PARTS
    vmem = pl.BlockSpec(memory_space=pltpu.VMEM)
    hbm = pl.BlockSpec(memory_space=pl.ANY)
    dma = pltpu.SemaphoreType.DMA
    return pl.pallas_call(
        functools.partial(kernel, n, own, rows, blocks),
        out_shape=jax.ShapeDtypeStruct((own, width), BF16),
        in_specs=[vmem, vmem, hbm, vmem, hbm, hbm, hbm],
        out_specs=vmem,
        scratch_shapes=[
            pltpu.VMEM(w_out.shape, BF16),
            pltpu.VMEM((width, units), BF16),
            pltpu.VMEM((width, units), BF16),
            pltpu.VMEM(w_down.shape, BF16),
            pltpu.VMEM((2 * n * per, BLOCK), F32),
            pltpu.VMEM((2, CHUNKS, n, per, BLOCK), BF16),
            pltpu.VMEM((2, CHUNKS, nh, per, BLOCK), BF16),
            pltpu.VMEM((2, CHUNKS, nh, per, BLOCK), BF16),
            pltpu.VMEM((2, CHUNKS, nq, per, BLOCK), BF16),
            pltpu.VMEM((2, CHUNKS, nq, per, BLOCK), BF16),
            pltpu.VMEM((2, CHUNKS, nq, per, BLOCK), BF16),
            pltpu.VMEM((own * blocks, BLOCK), F32),
            pltpu.VMEM((own * blocks, BLOCK), F32),
            pltpu.VMEM((PARTS, n, piece, BLOCK), BF16),
            pltpu.VMEM((rows * blocks, BLOCK), F32),
            dma((CHUNKS + 3,)),
            dma((2, CHUNKS)), dma((2, CHUNKS)),
            dma((2, CHUNKS)), dma((2, CHUNKS)),
            dma((2, CHUNKS, nq)), dma((2, CHUNKS, nq)),
            dma((PARTS, nq)), dma((PARTS, nq)),
            dma((PARTS, nq)), dma((PARTS, nq)),
            dma((PARTS, nh)), dma((PARTS, nh)),
        ],
        compiler_params=pltpu.CompilerParams(
            collective_id=0, has_side_effects=True, vmem_limit_bytes=60 * 1024 * 1024
        ),
    )(residual, context, w_out, ffn_gain.reshape(blocks, BLOCK), w_gate, w_up, w_down)


def solution(mesh):
    return jax.shard_map(
        local,
        mesh=mesh,
        in_specs=(
            P(("groups", "tensor"), None),
            P("groups", "tensor"),
            P("tensor", None),
            P(),
            P(None, "tensor"),
            P(None, "tensor"),
            P("tensor", None),
        ),
        out_specs=P(("groups", "tensor"), None),
        check_vma=False,
    )
```

time: 142 us -> 56.9 us (0.40)
  Pallas kernels: 0 us -> 42.6 us
  blocking collectives: 38.8 us -> 0 us
  waiting for transfers between devices: 26.2 us -> 0 us
  starting transfers between devices: 21.3 us -> 0 us
  matrix products: 16.8 us -> 0 us
  local copies, waits for them, and re-layouts: 27.7 us -> 13.9 us
  other arithmetic: 9.8 us -> 0 us
    pallas_call x0 -> x1, Pallas kernels: none -> 42.6 us  [local(): pl.pallas_call(functools.partial(kernel, n, own, rows, blocks), out_shape...]
    all_gather x2 -> x0, blocking collectives: 38.8 us -> none  [the longest x1 21.3 us: local(): lax.all_gather(norm_values, 'tensor', axis=0, tiled=True)]
    all_to_all x4 -> x0, waiting for transfers between devices: 26.2 us -> none  [the longest x1 11.3 us: local(): lax.all_to_all(code_values.reshape(axis_count, own_rows, model_width), 't...]
    all_to_all x4 -> x0, starting transfers between devices: 21.3 us -> none  [the longest x1 7.39 us: local(): lax.all_to_all(code_scales.reshape(axis_count, own_rows, -1), 'tensor', s...]
    dot_general x14 -> x0, matrix products: 16.8 us -> none  [the longest x1 6.72 us: ffn_partial(): return jnp.dot(hidden, w_down, preferred_element_type=jnp.float32)]
    unnamed x16 -> x3, local copies, waits for them, and re-layouts: 1.77 us -> 13.9 us
    mul x6 -> x0, local copies, waits for them, and re-layouts: 8.98 us -> none  [the longest x4 6.27 us: dequant(): return reshaped * code_scales.astype(jnp.float32)[..., None]]
    div x4 -> x0, local copies, waits for them, and re-layouts: 8.27 us -> none  [encode(): turned / code_scales.astype(jnp.float32)[..., None]]
  transfers between devices with their start and end apart: 4 -> 0, of which waited for: 3 -> 0; matrix products, arithmetic and copies ran while one was open for 14% -> 0% of each run, Pallas kernels for 0% -> 0%
where the time goes in v1:
time: 56.9 us; the launch traced here: 56.5 us
  Pallas kernels  42.6 us (75%)
  local copies, waits for them, and re-layouts  13.9 us (24%)
    pallas_call x1, Pallas kernels, local(): pl.pallas_call(functools.partial(kernel, n, own, rows, blocks), out_shape...  42.6 us
    unnamed x3, local copies, waits for them, and re-layouts  13.9 us

profile of v1, /device:TPU:0, one launch (start us, length us, event | category | flops | bytes accessed | tf_op | source)
XLA Modules:
  0.0 56.5 jit_solution(15611151331914364375)
XLA Ops:
  0.0 6.3 %copy.8.wg_hbm = bf16[8192,224]{1,0:T(8,128)(2,1)} copy(bf16[8192,224]{0,1:T(8,128)(2,1)} %param.11) | data formatting | bytes 7340032 | tf_op args[4]
  6.3 6.2 %copy.9.wu_hbm = bf16[8192,224]{1,0:T(8,128)(2,1)} copy(bf16[8192,224]{0,1:T(8,128)(2,1)} %param.12) | data formatting | bytes 7340032 | tf_op args[5]
  12.5 42.6 %shard_map.73 = bf16[2,8192]{1,0:T(2,128)(2,1)} custom-call(bf16[2,8192]{1,0:T(2,128)(2,1)} %res_ref.1, bf16[32,128]{1,0:T(8,128)(2,1)} %ctx_ref.1, bf16[128,8192]{1,0:T(8,128)(2,1)} %wo_hbm.1, bf16[64,128]{1,0:T(8,128)(2,1)} %bitcast.1, bf16[8192,224]{1,0:T(8,128)(2,1)} %copy.8.wg_hbm, bf16[8192,224]{1,0:T(8,128)(2,1)} %copy.9.wu_hbm, bf16[224,8192]{1,0:T(8,128)(2,1)} %wd_hbm.1), custom_call_target="tpu_custom_call" | custom-call | tf_op jit(solution)/shard_map/pallas_call | solution.py:224
  55.1 1.4 %copy.11 = bf16[2,8192]{1,0:T(2,128)(2,1)} copy(bf16[2,8192]{1,0:T(2,128)(2,1)} %shard_map.73) | data formatting | bytes 65536

commit v2 on v1

--- a/solution.py
+++ b/solution.py
@@ -17,6 +17,7 @@
 MESH = pl.DeviceIdType.MESH
 F32 = jnp.float32
 BF16 = jnp.bfloat16
+NT = (((1,), (1,)), ((), ()))
 ROOT = 1.0 / math.sqrt(BLOCK)
 
 
@@ -190,8 +191,8 @@
                 [lhs[pl.ds(base + b, rows, stride=bpc), :].astype(BF16) for b in range(bpc)], axis=1
             )
             span = pl.ds(k * cw, cw)
-            g_part = jnp.dot(left, wg[span, :], preferred_element_type=F32)
-            u_part = jnp.dot(left, wu[span, :], preferred_element_type=F32)
+            g_part = lax.dot_general(left, wg[:, span], NT, preferred_element_type=F32)
+            u_part = lax.dot_general(left, wu[:, span], NT, preferred_element_type=F32)
             gate = g_part if gate is None else gate + g_part
             up = u_part if up is None else up + u_part
     hidden = (gate / (1.0 + jnp.exp(-gate)) * up).astype(BF16)
@@ -228,8 +229,8 @@
         out_specs=vmem,
         scratch_shapes=[
             pltpu.VMEM(w_out.shape, BF16),
-            pltpu.VMEM((width, units), BF16),
-            pltpu.VMEM((width, units), BF16),
+            pltpu.VMEM((units, width), BF16),
+            pltpu.VMEM((units, width), BF16),
             pltpu.VMEM(w_down.shape, BF16),
             pltpu.VMEM((2 * n * per, BLOCK), F32),
             pltpu.VMEM((2, CHUNKS, n, per, BLOCK), BF16),
@@ -253,7 +254,7 @@
         compiler_params=pltpu.CompilerParams(
             collective_id=0, has_side_effects=True, vmem_limit_bytes=60 * 1024 * 1024
         ),
-    )(residual, context, w_out, ffn_gain.reshape(blocks, BLOCK), w_gate, w_up, w_down)
+    )(residual, context, w_out, ffn_gain.reshape(blocks, BLOCK), w_gate.T, w_up.T, w_down)
 
 
 def solution(mesh):

time: 56.9 us -> 45.1 us (0.79)
  local copies, waits for them, and re-layouts: 13.9 us -> 1.4 us
  Pallas kernels: 42.6 us -> 43.4 us
    unnamed x3 -> x1, local copies, waits for them, and re-layouts: 13.9 us -> 1.4 us
    pallas_call x1, Pallas kernels: 42.6 us -> 43.4 us  [local(): pl.pallas_call(functools.partial(kernel, n, own, rows, blocks), out_shape...]
where the time goes in v2:
time: 45.1 us; the launch traced here: 44.8 us
  Pallas kernels  43.4 us (96%)
  local copies, waits for them, and re-layouts  1.4 us (3%)
    pallas_call x1, Pallas kernels, local(): pl.pallas_call(functools.partial(kernel, n, own, rows, blocks), out_shape...  43.4 us
    unnamed x1, local copies, waits for them, and re-layouts  1.4 us

profile of v2, /device:TPU:0, one launch (start us, length us, event | category | flops | bytes accessed | tf_op | source)
XLA Modules:
  0.0 44.8 jit_solution(4271911895639618695)
XLA Ops:
  0.0 43.4 %shard_map.73 = bf16[2,8192]{1,0:T(2,128)(2,1)} custom-call(bf16[2,8192]{1,0:T(2,128)(2,1)} %res_ref.1, bf16[32,128]{1,0:T(8,128)(2,1)} %ctx_ref.1, bf16[128,8192]{1,0:T(8,128)(2,1)} %wo_hbm.1, bf16[64,128]{1,0:T(8,128)(2,1)} %bitcast.5, bf16[224,8192]{1,0:T(8,128)(2,1)} %bitcast.3, bf16[224,8192]{1,0:T(8,128)(2,1)} %bitcast.4, bf16[224,8192]{1,0:T(8,128)(2,1)} %wd_hbm.1), custom_call_target="tpu_custom_call" | custom-call | tf_op jit(solution)/shard_map/pallas_call | solution.py:225
  43.4 1.4 %copy.9 = bf16[2,8192]{1,0:T(2,128)(2,1)} copy(bf16[2,8192]{1,0:T(2,128)(2,1)} %shard_map.73) | data formatting | bytes 65536

commit v3 on v2

--- a/solution.py
+++ b/solution.py
@@ -25,25 +25,23 @@
     n, own, rows, blocks,
     res_ref, ctx_ref, wo_hbm, gain_ref, wg_hbm, wu_hbm, wd_hbm,
     out_ref,
-    wo, wg, wu, wd, turn, s1, r1, s2, r2, s3, r3, resid, mid_ref, gath, lhs,
-    wsem, s1s, s1r, s2s, s2r, s3s, s3r, gzs, gzr, gys, gyr, gcs, gcr,
+    wo, wg, wu, wd, turn, s1, r1, s2, r2, resid, mid_ref, gath, lhs,
+    wsem, s1s, s1r, s2s, s2r, gds, gdr, gcs, gcr,
 ):
-    nh, nq = n // 2, n // 4
+    nh = n // 2
     bpc = blocks // CHUNKS
     cw = bpc * BLOCK
     per = own * bpc
     me = lax.axis_index("tensor")
     c = lax.rem(me, 2)
-    y = lax.rem(me // 2, 2)
-    q = me // 4
+    chip = me // 2
     core_dev = me + 1 - 2 * c
-    y_dev = me + 2 - 4 * y
-
-    def z_dev(k):
-        return lax.rem(q + k, nq) * 4 + y * 2 + c
-
-    def z_src(k):
-        return lax.rem(q + nq - k, nq)
+
+    def far(k):
+        return lax.rem(chip + k, nh) * 2 + c
+
+    def source(k):
+        return lax.rem(chip + nh - k, nh) * 2 + c
 
     wcopies = []
     for k in range(CHUNKS):
@@ -56,7 +54,7 @@
         cp.start()
 
     barrier = pltpu.get_barrier_semaphore()
-    for dev in [core_dev, y_dev] + [z_dev(k) for k in range(1, nq)]:
+    for dev in [core_dev] + [far(k) for k in range(1, nh)]:
         pl.semaphore_signal(barrier, inc=1, device_id={"tensor": dev}, device_id_type=MESH)
 
     par = lax.broadcasted_iota(jnp.int32, (2 * BLOCK, BLOCK), 0) & lax.broadcasted_iota(
@@ -100,39 +98,33 @@
         for b in range(bpc):
             turn[pl.ds(base + b, rows, stride=bpc), :] = v[b * rows:(b + 1) * rows]
         for t in range(n):
-            slot = (t % 2) * nh + (t // 2 % 2) * nq + t // 4
+            slot = (t % 2) * nh + t // 2
             s1[p, k, slot] = turn[base + t * per:base + (t + 1) * per, :].astype(BF16)
 
     def reduce_scatter(p, left, w, before):
-        c1, c2, c3 = {}, {}, {}
-        for step in range(CHUNKS + 2):
+        c1, c2 = {}, {}
+        for step in range(CHUNKS + 1):
             k = step
             if k < CHUNKS:
                 before(k)
                 term(p, k, left, w)
                 if p == 0 and k == 0:
-                    pl.semaphore_wait(barrier, 1 + nq)
+                    pl.semaphore_wait(barrier, nh)
                 c1[k] = remote(s1.at[p, k, pl.ds((1 - c) * nh, nh)], r1.at[p, k],
                                s1s.at[p, k], s1r.at[p, k], core_dev)
             k = step - 1
-            if 0 <= k < CHUNKS:
+            if k >= 0:
                 c1[k].wait_recv()
                 s2[p, k] = (s1[p, k, pl.ds(c * nh, nh)].astype(F32) + r1[p, k].astype(F32)).astype(BF16)
-                c2[k] = remote(s2.at[p, k, pl.ds((1 - y) * nq, nq)], r2.at[p, k],
-                               s2s.at[p, k], s2r.at[p, k], y_dev)
-            k = step - 2
-            if 0 <= k < CHUNKS:
-                c2[k].wait_recv()
-                s3[p, k] = (s2[p, k, pl.ds(y * nq, nq)].astype(F32) + r2[p, k].astype(F32)).astype(BF16)
-                for j in range(1, nq):
-                    c3[k, j] = remote(s3.at[p, k, lax.rem(q + j, nq)], r3.at[p, k, j],
-                                      s3s.at[p, k, j], s3r.at[p, k, j], z_dev(j))
+                for j in range(1, nh):
+                    c2[k, j] = remote(s2.at[p, k, lax.rem(chip + j, nh)], r2.at[p, k, j],
+                                      s2s.at[p, k, j], s2r.at[p, k, j], far(j))
         totals = []
         for k in range(CHUNKS):
-            total = s3[p, k, q].astype(F32)
-            for j in range(1, nq):
-                c3[k, j].wait_recv()
-                total = total + r3[p, k, j].astype(F32)
+            total = s2[p, k, chip].astype(F32)
+            for j in range(1, nh):
+                c2[k, j].wait_recv()
+                total = total + r2[p, k, j].astype(F32)
             totals.append(total)
         return jnp.concatenate(totals, axis=0)
 
@@ -153,40 +145,38 @@
     normed = (mid4 * inverse[None] * gain).reshape(blocks * own, BLOCK)
     ffn_in = jnp.dot(coded(normed).astype(BF16), had, preferred_element_type=F32) * ROOT
     piece = own * blocks // PARTS
-    cz, cy, cc = {}, {}, {}
+    cd, cc = {}, {}
+    group = CHUNKS // PARTS
 
     def share(a, slot, dev, ss, rs, i):
         return remote(gath.at[a, slot], gath.at[a, slot], ss.at[a, i], rs.at[a, i], dev)
 
+    def place(a, slot):
+        for g in range(group):
+            start = pl.multiple_of((a * group + g) * rows * bpc + slot * per, per)
+            lhs[pl.ds(start, per), :] = gath[a, slot, g * per:(g + 1) * per, :].astype(F32)
+
     for a in range(PARTS):
         gath[a, me] = ffn_in[a * piece:(a + 1) * piece].astype(BF16)
-        for k in range(1, nq):
-            cz[a, k] = share(a, me, z_dev(k), gzs, gzr, k)
-        cy[a, 0] = share(a, me, y_dev, gys, gyr, 0)
+        for k in range(1, nh):
+            cd[a, k] = share(a, me, far(k), gds, gdr, k)
         cc[a, 0] = share(a, me, core_dev, gcs, gcr, 0)
     for a in range(PARTS):
-        for k in range(1, nq):
-            cz[a, k].wait_recv()
-            slot = z_src(k) * 4 + y * 2 + c
-            cy[a, k] = share(a, slot, y_dev, gys, gyr, k)
-            cc[a, k] = share(a, slot, core_dev, gcs, gcr, k)
-    for a in range(PARTS):
-        for k in range(nq):
-            cy[a, k].wait_recv()
-            slot = z_src(k) * 4 + (1 - y) * 2 + c
-            cc[a, nq + k] = share(a, slot, core_dev, gcs, gcr, nq + k)
+        place(a, me)
+        for k in range(1, nh):
+            cd[a, k].wait_recv()
+            cc[a, k] = share(a, source(k), core_dev, gcs, gcr, k)
+            place(a, source(k))
     wcopies[CHUNKS].wait()
     wcopies[CHUNKS + 1].wait()
     gate = up = None
-    group = CHUNKS // PARTS
     for a in range(PARTS):
         for k in range(nh):
             cc[a, k].wait_recv()
+            place(a, source(k) + 1 - 2 * c)
         for g in range(group):
             k = a * group + g
             base = k * rows * bpc
-            for t in range(n):
-                lhs[base + t * per:base + (t + 1) * per, :] = gath[a, t, g * per:(g + 1) * per, :].astype(F32)
             left = jnp.concatenate(
                 [lhs[pl.ds(base + b, rows, stride=bpc), :].astype(BF16) for b in range(bpc)], axis=1
             )
@@ -216,7 +206,7 @@
     rows = context.shape[0]
     blocks = width // BLOCK
     units = w_gate.shape[1]
-    nh, nq = n // 2, n // 4
+    nh = n // 2
     per = own * blocks // CHUNKS
     piece = own * blocks // PARTS
     vmem = pl.BlockSpec(memory_space=pltpu.VMEM)
@@ -236,19 +226,15 @@
             pltpu.VMEM((2, CHUNKS, n, per, BLOCK), BF16),
             pltpu.VMEM((2, CHUNKS, nh, per, BLOCK), BF16),
             pltpu.VMEM((2, CHUNKS, nh, per, BLOCK), BF16),
-            pltpu.VMEM((2, CHUNKS, nq, per, BLOCK), BF16),
-            pltpu.VMEM((2, CHUNKS, nq, per, BLOCK), BF16),
-            pltpu.VMEM((2, CHUNKS, nq, per, BLOCK), BF16),
+            pltpu.VMEM((2, CHUNKS, nh, per, BLOCK), BF16),
             pltpu.VMEM((own * blocks, BLOCK), F32),
             pltpu.VMEM((own * blocks, BLOCK), F32),
             pltpu.VMEM((PARTS, n, piece, BLOCK), BF16),
             pltpu.VMEM((rows * blocks, BLOCK), F32),
             dma((CHUNKS + 3,)),
             dma((2, CHUNKS)), dma((2, CHUNKS)),
-            dma((2, CHUNKS)), dma((2, CHUNKS)),
-            dma((2, CHUNKS, nq)), dma((2, CHUNKS, nq)),
-            dma((PARTS, nq)), dma((PARTS, nq)),
-            dma((PARTS, nq)), dma((PARTS, nq)),
+            dma((2, CHUNKS, nh)), dma((2, CHUNKS, nh)),
+            dma((PARTS, nh)), dma((PARTS, nh)),
             dma((PARTS, nh)), dma((PARTS, nh)),
         ],
         compiler_params=pltpu.CompilerParams(

time: 45.1 us -> 39.7 us (0.88)
  Pallas kernels: 43.4 us -> 38.1 us
    pallas_call x1, Pallas kernels: 43.4 us -> 38.1 us  [local(): pl.pallas_call(functools.partial(kernel, n, own, rows, blocks), out_shape...]
where the time goes in v3:
time: 39.7 us; the launch traced here: 39.5 us
  Pallas kernels  38.1 us (96%)
  local copies, waits for them, and re-layouts  1.4 us (4%)
    pallas_call x1, Pallas kernels, local(): pl.pallas_call(functools.partial(kernel, n, own, rows, blocks), out_shape...  38.1 us
    unnamed x1, local copies, waits for them, and re-layouts  1.4 us

profile of v3, /device:TPU:0, one launch (start us, length us, event | category | flops | bytes accessed | tf_op | source)
XLA Modules:
  0.0 39.5 jit_solution(16654269049422616122)
XLA Ops:
  0.0 38.1 %shard_map.73 = bf16[2,8192]{1,0:T(2,128)(2,1)} custom-call(bf16[2,8192]{1,0:T(2,128)(2,1)} %res_ref.1, bf16[32,128]{1,0:T(8,128)(2,1)} %ctx_ref.1, bf16[128,8192]{1,0:T(8,128)(2,1)} %wo_hbm.1, bf16[64,128]{1,0:T(8,128)(2,1)} %bitcast.5, bf16[224,8192]{1,0:T(8,128)(2,1)} %bitcast.3, bf16[224,8192]{1,0:T(8,128)(2,1)} %bitcast.4, bf16[224,8192]{1,0:T(8,128)(2,1)} %wd_hbm.1), custom_call_target="tpu_custom_call" | custom-call | tf_op jit(solution)/shard_map/pallas_call | solution.py:215
  38.1 1.4 %copy.9 = bf16[2,8192]{1,0:T(2,128)(2,1)} copy(bf16[2,8192]{1,0:T(2,128)(2,1)} %shard_map.73) | data formatting | bytes 65536

commit v4 on v3

--- a/solution.py
+++ b/solution.py
@@ -18,14 +18,20 @@
 F32 = jnp.float32
 BF16 = jnp.bfloat16
 NT = (((1,), (1,)), ((), ()))
+
+
+def partner_order(count):
+    return range(count - 1, 0, -1)
+
+
 ROOT = 1.0 / math.sqrt(BLOCK)
 
 
 def kernel(
     n, own, rows, blocks,
-    res_ref, ctx_ref, wo_hbm, gain_ref, wg_hbm, wu_hbm, wd_hbm,
+    res_hbm, ctx_hbm, wo_hbm, gain_hbm, wg_hbm, wu_hbm, wd_hbm,
     out_ref,
-    wo, wg, wu, wd, turn, s1, r1, s2, r2, resid, mid_ref, gath, lhs,
+    res_ref, ctx_ref, gain_ref, wo, wg, wu, wd, turn, s1, r1, s2, r2, resid, mid_ref, gath, lhs,
     wsem, s1s, s1r, s2s, s2r, gds, gdr, gcs, gcr,
 ):
     nh = n // 2
@@ -37,12 +43,27 @@
     chip = me // 2
     core_dev = me + 1 - 2 * c
 
+    def flip(k):
+        other, bit = chip, 1
+        while bit < nh:
+            if k & bit:
+                other = other + bit * (1 - 2 * lax.rem(chip // bit, 2))
+            bit *= 2
+        return other
+
     def far(k):
-        return lax.rem(chip + k, nh) * 2 + c
-
-    def source(k):
-        return lax.rem(chip + nh - k, nh) * 2 + c
-
+        return flip(k) * 2 + c
+
+    source = far
+
+    barrier = pltpu.get_barrier_semaphore()
+    for dev in [core_dev] + [far(k) for k in partner_order(nh)]:
+        pl.semaphore_signal(barrier, inc=1, device_id={"tensor": dev}, device_id_type=MESH)
+
+    small = []
+    for i, (src, dst) in enumerate(((ctx_hbm, ctx_ref), (res_hbm, res_ref), (gain_hbm, gain_ref))):
+        small.append(pltpu.make_async_copy(src, dst, wsem.at[CHUNKS + 3 + i]))
+    small[0].start()
     wcopies = []
     for k in range(CHUNKS):
         cols = pl.ds(k * cw, cw)
@@ -50,12 +71,8 @@
     wcopies.append(pltpu.make_async_copy(wg_hbm, wg, wsem.at[CHUNKS]))
     wcopies.append(pltpu.make_async_copy(wu_hbm, wu, wsem.at[CHUNKS + 1]))
     wcopies.append(pltpu.make_async_copy(wd_hbm, wd, wsem.at[CHUNKS + 2]))
-    for cp in wcopies:
+    for cp in wcopies[:CHUNKS] + small[1:]:
         cp.start()
-
-    barrier = pltpu.get_barrier_semaphore()
-    for dev in [core_dev] + [far(k) for k in range(1, nh)]:
-        pl.semaphore_signal(barrier, inc=1, device_id={"tensor": dev}, device_id_type=MESH)
 
     par = lax.broadcasted_iota(jnp.int32, (2 * BLOCK, BLOCK), 0) & lax.broadcasted_iota(
         jnp.int32, (2 * BLOCK, BLOCK), 1
@@ -101,7 +118,7 @@
             slot = (t % 2) * nh + t // 2
             s1[p, k, slot] = turn[base + t * per:base + (t + 1) * per, :].astype(BF16)
 
-    def reduce_scatter(p, left, w, before):
+    def reduce_scatter(p, left, w, before, between):
         c1, c2 = {}, {}
         for step in range(CHUNKS + 1):
             k = step
@@ -116,9 +133,10 @@
             if k >= 0:
                 c1[k].wait_recv()
                 s2[p, k] = (s1[p, k, pl.ds(c * nh, nh)].astype(F32) + r1[p, k].astype(F32)).astype(BF16)
-                for j in range(1, nh):
-                    c2[k, j] = remote(s2.at[p, k, lax.rem(chip + j, nh)], r2.at[p, k, j],
+                for j in partner_order(nh):
+                    c2[k, j] = remote(s2.at[p, k, flip(j)], r2.at[p, k, j],
                                       s2s.at[p, k, j], s2r.at[p, k, j], far(j))
+        between()
         totals = []
         for k in range(CHUNKS):
             total = s2[p, k, chip].astype(F32)
@@ -130,12 +148,19 @@
 
     def before_out(k):
         wcopies[k].wait()
-
-    res = res_ref[...].astype(F32)
-    for b in range(blocks):
-        resid[pl.ds((b // bpc) * per + b % bpc, own, stride=bpc), :] = res[:, b * BLOCK:(b + 1) * BLOCK]
-
-    attn = reduce_scatter(0, ctx_ref[...], wo, before_out)
+        if k == CHUNKS - 1:
+            for cp in wcopies[CHUNKS:]:
+                cp.start()
+
+    def spread_residual():
+        small[1].wait()
+        small[2].wait()
+        res = res_ref[...].astype(F32)
+        for b in range(blocks):
+            resid[pl.ds((b // bpc) * per + b % bpc, own, stride=bpc), :] = res[:, b * BLOCK:(b + 1) * BLOCK]
+
+    small[0].wait()
+    attn = reduce_scatter(0, ctx_ref[...], wo, before_out, spread_residual)
     mid = (resid[...] + rotate(attn)).astype(BF16).astype(F32)
     mid_ref[...] = mid
     mid4 = mid.reshape(CHUNKS, own, bpc, BLOCK)
@@ -158,7 +183,7 @@
 
     for a in range(PARTS):
         gath[a, me] = ffn_in[a * piece:(a + 1) * piece].astype(BF16)
-        for k in range(1, nh):
+        for k in partner_order(nh):
             cd[a, k] = share(a, me, far(k), gds, gdr, k)
         cc[a, 0] = share(a, me, core_dev, gcs, gcr, 0)
     for a in range(PARTS):
@@ -191,7 +216,7 @@
         if k == 0:
             wcopies[CHUNKS + 2].wait()
 
-    ffn = reduce_scatter(1, hidden, wd, before_down)
+    ffn = reduce_scatter(1, hidden, wd, before_down, lambda: None)
     resid[...] = mid_ref[...] + rotate(ffn)
     for b in range(blocks):
         row = resid[pl.ds((b // bpc) * per + b % bpc, own, stride=bpc), :]
@@ -215,9 +240,12 @@
     return pl.pallas_call(
         functools.partial(kernel, n, own, rows, blocks),
         out_shape=jax.ShapeDtypeStruct((own, width), BF16),
-        in_specs=[vmem, vmem, hbm, vmem, hbm, hbm, hbm],
+        in_specs=[hbm] * 7,
         out_specs=vmem,
         scratch_shapes=[
+            pltpu.VMEM(residual.shape, BF16),
+            pltpu.VMEM(context.shape, BF16),
+            pltpu.VMEM((blocks, BLOCK), BF16),
             pltpu.VMEM(w_out.shape, BF16),
             pltpu.VMEM((units, width), BF16),
             pltpu.VMEM((units, width), BF16),
@@ -231,7 +259,7 @@
             pltpu.VMEM((own * blocks, BLOCK), F32),
             pltpu.VMEM((PARTS, n, piece, BLOCK), BF16),
             pltpu.VMEM((rows * blocks, BLOCK), F32),
-            dma((CHUNKS + 3,)),
+            dma((CHUNKS + 6,)),
             dma((2, CHUNKS)), dma((2, CHUNKS)),
             dma((2, CHUNKS, nh)), dma((2, CHUNKS, nh)),
             dma((PARTS, nh)), dma((PARTS, nh)),

time: 39.7 us -> 39 us (0.982)
  Pallas kernels: 38.1 us -> 37.4 us
    pallas_call x1, Pallas kernels: 38.1 us -> 37.4 us  [local(): pl.pallas_call(functools.partial(kernel, n, own, rows, blocks), out_shape...]
where the time goes in v4:
time: 39 us; the launch traced here: 38.8 us
  Pallas kernels  37.4 us (96%)
  local copies, waits for them, and re-layouts  1.4 us (4%)
    pallas_call x1, Pallas kernels, local(): pl.pallas_call(functools.partial(kernel, n, own, rows, blocks), out_shape...  37.4 us
    unnamed x1, local copies, waits for them, and re-layouts  1.4 us

profile of v4, /device:TPU:0, one launch (start us, length us, event | category | flops | bytes accessed | tf_op | source)
XLA Modules:
  0.0 38.8 jit_solution(15899604543451382345)
XLA Ops:
  0.0 37.4 %shard_map.73 = bf16[2,8192]{1,0:T(2,128)(2,1)} custom-call(bf16[2,8192]{1,0:T(2,128)(2,1)} %res_hbm.1, bf16[32,128]{1,0:T(8,128)(2,1)} %ctx_hbm.1, bf16[128,8192]{1,0:T(8,128)(2,1)} %wo_hbm.1, bf16[64,128]{1,0:T(8,128)(2,1)} %bitcast.5, bf16[224,8192]{1,0:T(8,128)(2,1)} %bitcast.3, bf16[224,8192]{1,0:T(8,128)(2,1)} %bitcast.4, bf16[224,8192]{1,0:T(8,128)(2,1)} %wd_hbm.1), custom_call_target="tpu_custom_call" | custom-call | tf_op jit(solution)/shard_map/pallas_call | solution.py:240
  37.4 1.4 %copy.9 = bf16[2,8192]{1,0:T(2,128)(2,1)} copy(bf16[2,8192]{1,0:T(2,128)(2,1)} %shard_map.73) | data formatting | bytes 65536
